TPU v7x, 32 devices: a whole 2x2x4 slice. The times are simulated.
32 devices in a mesh: tm: 8 (over y, x, core), space: 4 (over z).
Axes of the slice: x: 2, y: 2, z: 4, core: 2. Of those that a mesh axis runs over, the one named last changes fastest.
Arguments:
- initial_state: float32 [64, 512], P(None, 'space'), may hold values from -6 to 6
- forcing: float32 [32, 64, 512], P('tm', None, 'space'), may hold values from -4 to 4
- coarse_gain: float32 [8, 64, 512], P('tm', None, 'space'), may hold values from 0.05 to 1, as said below
- block_inverse: float32 [64, 64, 512], P(None, None, 'space'), may hold values from -0.25 to 1.1
- face_blocks: float32 [6, 64, 64], replicated, may hold values from -0.1875 to 0.1875
- neighbor: int32 [6, 512], P(None, 'space'), may hold values from -1 to 255, as said below
- send_rows: int32 [2, 256], P(None, 'space'), may hold values from 0 to 127, as said below
Outputs:
- coarse_end: float32 [8, 64, 512], P('tm', None, 'space')
- residual: float32 [8, 64, 512], P('tm', None, 'space')
Inputs may be any that keep to these rules, and one draw needn't show every extreme that they name: `neighbor`: for face f (-x, +x, -y, +y, -z, +z) of the element in local column e, the local column of its neighbour in the extended field of its partition; -1 where the face lies on the domain's side along x or y. `send_rows`: row 0 lists the local columns of a partition's lowest element layer, row 1 those of its highest, in the same order of x and y. `coarse_gain`: Positive, below one.
All inputs are finite; a program needn't handle non-finite values.
Results may differ from a plain program's by a relative error of at most 0.00014.
Values sent between devices are 32-bit elements; how exact they have to be, the bound alone decides.
A program may use at most 64 MiB of HBM per device.

v0:
```python
import jax
import jax.numpy as jnp
from jax import lax
from jax.sharding import PartitionSpec as P

STEPS = 4
SWEEPS = 2
ITERS = 2


HIGHEST_PRECISION = lax.Precision.HIGHEST


def extended_2(cells, sides, width):
    for axis, dim in sides:
        count = lax.axis_size(axis)
        ends = count - 1
        head = lax.slice_in_dim(cells, 0, width, axis=dim)
        tail = lax.slice_in_dim(cells, cells.shape[dim] - width, cells.shape[dim], axis=dim)
        cells = jnp.concatenate(
            [
                lax.ppermute(tail, axis, [(i, (i + 1) % count) for i in range(ends)]),
                cells,
                lax.ppermute(head, axis, [((i + 1) % count, i) for i in range(ends)]),
            ],
            axis=dim,
        )
    return cells


def shifted(x, axis, by):
    size = lax.axis_size(axis)
    pairs = [(i, i + by) for i in range(size) if 0 <= i + by < size]
    return lax.ppermute(x, axis, pairs)


def carried_in(part, axis, combine, identity):
    place = lax.axis_index(axis)
    gathered = jax.tree.map(lambda a: lax.all_gather(a, axis), part)
    state = jax.tree.map(lambda a, e: jnp.zeros_like(a) + jnp.asarray(e, a.dtype), part, identity)

    def one(lap, state):
        return combine(
            state, jax.tree.map(lambda a: lax.dynamic_index_in_dim(a, lap, 0, False), gathered)
        )

    return lax.fori_loop(0, place, one, state)


def apply_inverse(block_inverse, vector):
    return jnp.einsum("ije,je->ie", block_inverse, vector, precision=HIGHEST_PRECISION)


def extend(field_now, send_rows):
    values = field_now.shape[0]
    layer_size = send_rows.shape[1]
    bottom = jnp.take(field_now, send_rows[0], axis=1)
    upper_rows = jnp.take(field_now, send_rows[1], axis=1)
    stacked = jnp.stack([bottom.reshape(-1), upper_rows.reshape(-1)], axis=0)
    padded = extended_2(stacked, (("space", 0),), 1)
    below_rows = padded[0].reshape(values, layer_size)
    above_rows = padded[3].reshape(values, layer_size)
    return jnp.concatenate([field_now, below_rows, above_rows], axis=1)


def coupling(field_now, face_blocks, neighbor, send_rows):
    extended = extend(field_now, send_rows)
    face_valid = (neighbor >= 0).astype(jnp.float32)
    picked = jnp.take(extended, jnp.maximum(neighbor, 0), axis=1) * face_valid[None]
    return jnp.einsum("fij,jfe->ie", face_blocks, picked, precision=HIGHEST_PRECISION)


def fine_step(field_now, source, block_inverse, face_blocks, neighbor, send_rows):
    right_side = field_now + source
    iterate = apply_inverse(block_inverse, right_side)
    for sweep_index in range(SWEEPS):
        iterate = apply_inverse(
            block_inverse, right_side - coupling(iterate, face_blocks, neighbor, send_rows)
        )
    return iterate


def compose(earlier, later):
    return (earlier[0] * later[0], later[0] * earlier[1] + later[1])


def body(initial_state, forcing, coarse_gain, block_inverse, face_blocks, neighbor, send_rows):
    gain_now = coarse_gain[0]
    slot_index = lax.axis_index("tm")
    first_slice = (slot_index == 0).astype(jnp.float32)
    coarse = jnp.zeros_like(initial_state)
    residual = coarse
    for iteration in range(ITERS):
        previous = shifted(coarse, "tm", 1)
        field_now = previous + first_slice * initial_state
        for step_index in range(STEPS):
            field_now = fine_step(
                field_now, forcing[step_index], block_inverse, face_blocks, neighbor, send_rows
            )
        residual = field_now - coarse
        prefix = carried_in(
            (gain_now, residual), "tm", compose, (jnp.ones_like(gain_now), jnp.zeros_like(residual))
        )
        correction = gain_now * prefix[1] + residual
        coarse = coarse + correction
    return (coarse[None], residual[None])


def solution(mesh):
    return jax.shard_map(
        body,
        mesh=mesh,
        in_specs=(
            P(None, "space"),
            P("tm", None, "space"),
            P("tm", None, "space"),
            P(None, None, "space"),
            P(),
            P(None, "space"),
            P(None, "space"),
        ),
        out_specs=(P("tm", None, "space"), P("tm", None, "space")),
        check_vma=False,
    )
```

profile of v0, /device:TPU:0, one launch (start us, length us, event | category | flops | bytes accessed | tf_op | source)
XLA Modules:
  0.0 254.9 jit_solution(27346232146568080)
XLA Ops:
  0.7 2.5 collective-permute-start
  6.1 1.9 multiply_reduce_fusion.23
  9.0 4.3 %collective-permute-start.1 = (f32[1,4096]{1,0:T(1,128)S(1)}, f32[1,4096]{1,0:T(1,128)S(1)}, u32[]{:S(2)}, u32[]{:S(2)}) collective-permute-start(f32[1,4096]{1,0:T(1,128)S(1)} %stack_reshape.96), channel_id=1, source_target_pairs={{0,1},{1,2},{2,3},{4,5},{5,6},{6,7},{8,9},{9,10},{10,11},{12,13},{... | collective-permute-start | bytes 49160 | tf_op jit(solution)/shard_map/ppermute | solution.py:22
  17.1 2.8 %collective-permute-done.2 = f32[1,4096]{1,0:T(1,128)S(1)} collective-permute-done((f32[1,4096]{1,0:T(1,128)S(1)}, f32[1,4096]{1,0:T(1,128)S(1)}, u32[]{:S(2)}, u32[]{:S(2)}) %collective-permute-start.2) | collective-permute-done | bytes 16416 | tf_op jit(solution)/shard_map/ppermute | solution.py:24
  24.9 3.5 %collective-permute-start.3 = (f32[1,4096]{1,0:T(1,128)S(1)}, f32[1,4096]{1,0:T(1,128)S(1)}, u32[]{:S(2)}, u32[]{:S(2)}) collective-permute-start(f32[1,4096]{1,0:T(1,128)S(1)} %stack_reshape.98), channel_id=1, source_target_pairs={{0,1},{1,2},{2,3},{4,5},{5,6},{6,7},{8,9},{9,10},{10,11},{12,13},{... | collective-permute-start | bytes 49160 | tf_op jit(solution)/shard_map/ppermute | solution.py:22
  30.8 3.4 %collective-permute-done.4 = f32[1,4096]{1,0:T(1,128)S(1)} collective-permute-done((f32[1,4096]{1,0:T(1,128)S(1)}, f32[1,4096]{1,0:T(1,128)S(1)}, u32[]{:S(2)}, u32[]{:S(2)}) %collective-permute-start.4) | collective-permute-done | bytes 16416 | tf_op jit(solution)/shard_map/ppermute | solution.py:24
  39.6 3.5 %collective-permute-start.5 = (f32[1,4096]{1,0:T(1,128)S(1)}, f32[1,4096]{1,0:T(1,128)S(1)}, u32[]{:S(2)}, u32[]{:S(2)}) collective-permute-start(f32[1,4096]{1,0:T(1,128)S(1)} %stack_reshape.100), channel_id=1, source_target_pairs={{0,1},{1,2},{2,3},{4,5},{5,6},{6,7},{8,9},{9,10},{10,11},{12,13},{... | collective-permute-start | bytes 49160 | tf_op jit(solution)/shard_map/ppermute | solution.py:22
  45.5 3.4 %collective-permute-done.6 = f32[1,4096]{1,0:T(1,128)S(1)} collective-permute-done((f32[1,4096]{1,0:T(1,128)S(1)}, f32[1,4096]{1,0:T(1,128)S(1)}, u32[]{:S(2)}, u32[]{:S(2)}) %collective-permute-start.6) | collective-permute-done | bytes 16416 | tf_op jit(solution)/shard_map/ppermute | solution.py:24
  53.8 1.9 collective-permute-start.7
  58.2 3.4 %collective-permute-done.8 = f32[1,4096]{1,0:T(1,128)S(1)} collective-permute-done((f32[1,4096]{1,0:T(1,128)S(1)}, f32[1,4096]{1,0:T(1,128)S(1)}, u32[]{:S(2)}, u32[]{:S(2)}) %collective-permute-start.8) | collective-permute-done | bytes 16416 | tf_op jit(solution)/shard_map/ppermute | solution.py:24
  66.9 1.9 collective-permute-start.9
  71.3 3.4 %collective-permute-done.10 = f32[1,4096]{1,0:T(1,128)S(1)} collective-permute-done((f32[1,4096]{1,0:T(1,128)S(1)}, f32[1,4096]{1,0:T(1,128)S(1)}, u32[]{:S(2)}, u32[]{:S(2)}) %collective-permute-start.10) | collective-permute-done | bytes 16416 | tf_op jit(solution)/shard_map/ppermute | solution.py:24
  79.6 1.9 collective-permute-start.11
  84.0 3.4 %collective-permute-done.12 = f32[1,4096]{1,0:T(1,128)S(1)} collective-permute-done((f32[1,4096]{1,0:T(1,128)S(1)}, f32[1,4096]{1,0:T(1,128)S(1)}, u32[]{:S(2)}, u32[]{:S(2)}) %collective-permute-start.12) | collective-permute-done | bytes 16416 | tf_op jit(solution)/shard_map/ppermute | solution.py:24
  97.2 3.3 %collective-permute-done.14 = f32[1,4096]{1,0:T(1,128)S(1)} collective-permute-done((f32[1,4096]{1,0:T(1,128)S(1)}, f32[1,4096]{1,0:T(1,128)S(1)}, u32[]{:S(2)}, u32[]{:S(2)}) %collective-permute-start.14) | collective-permute-done | bytes 16416 | tf_op jit(solution)/shard_map/ppermute | solution.py:24
  105.4 1.9 collective-permute-start.15
  108.9 11.5 %all_gather.16 = f32[8,64,128]{2,1,0:T(8,128)S(1)} all-gather(f32[1,64,128]{2,1,0:T(8,128)S(1)} %copy-done.4), channel_id=1, replica_groups=mesh['tm'=8,'space'=4] {'tm'}, dimensions={0}, use_global_device_ids=true | all-gather | bytes 294912 | tf_op jit(solution)/shard_map/all_gather | solution.py:39
  124.6 8.4 %all-gather = f32[512,128]{1,0:T(8,128)S(1)} all-gather(f32[64,128]{1,0:T(8,128)S(1)} %bitcast.609), channel_id=2, replica_groups=mesh['tm'=8,'space'=4] {'tm'}, dimensions={0}, use_global_device_ids=true | all-gather | bytes 294912 | tf_op jit(solution)/shard_map/all_gather | solution.py:39
  133.0 2.3 collective-permute-start.17
  138.1 4.5 %collective-permute-start.18 = (f32[1,4096]{1,0:T(1,128)S(1)}, f32[1,4096]{1,0:T(1,128)S(1)}, u32[]{:S(2)}, u32[]{:S(2)}) collective-permute-start(f32[1,4096]{1,0:T(1,128)S(1)} %stack_reshape.112), channel_id=1, source_target_pairs={{0,1},{1,2},{2,3},{4,5},{5,6},{6,7},{8,9},{9,10},{10,11},{12,13},{... | collective-permute-start | bytes 49160 | tf_op jit(solution)/shard_map/ppermute | solution.py:22
  145.1 3.5 %collective-permute-done.19 = f32[1,4096]{1,0:T(1,128)S(1)} collective-permute-done((f32[1,4096]{1,0:T(1,128)S(1)}, f32[1,4096]{1,0:T(1,128)S(1)}, u32[]{:S(2)}, u32[]{:S(2)}) %collective-permute-start.19) | collective-permute-done | bytes 16416 | tf_op jit(solution)/shard_map/ppermute | solution.py:24
  157.8 3.4 %collective-permute-done.21 = f32[1,4096]{1,0:T(1,128)S(1)} collective-permute-done((f32[1,4096]{1,0:T(1,128)S(1)}, f32[1,4096]{1,0:T(1,128)S(1)}, u32[]{:S(2)}, u32[]{:S(2)}) %collective-permute-start.21) | collective-permute-done | bytes 16416 | tf_op jit(solution)/shard_map/ppermute | solution.py:24
  166.5 1.9 collective-permute-start.22
  170.9 3.4 %collective-permute-done.23 = f32[1,4096]{1,0:T(1,128)S(1)} collective-permute-done((f32[1,4096]{1,0:T(1,128)S(1)}, f32[1,4096]{1,0:T(1,128)S(1)}, u32[]{:S(2)}, u32[]{:S(2)}) %collective-permute-start.23) | collective-permute-done | bytes 16416 | tf_op jit(solution)/shard_map/ppermute | solution.py:24
  179.2 1.9 collective-permute-start.24
  183.6 3.4 %collective-permute-done.25 = f32[1,4096]{1,0:T(1,128)S(1)} collective-permute-done((f32[1,4096]{1,0:T(1,128)S(1)}, f32[1,4096]{1,0:T(1,128)S(1)}, u32[]{:S(2)}, u32[]{:S(2)}) %collective-permute-start.25) | collective-permute-done | bytes 16416 | tf_op jit(solution)/shard_map/ppermute | solution.py:24
  196.9 3.2 %collective-permute-done.27 = f32[1,4096]{1,0:T(1,128)S(1)} collective-permute-done((f32[1,4096]{1,0:T(1,128)S(1)}, f32[1,4096]{1,0:T(1,128)S(1)}, u32[]{:S(2)}, u32[]{:S(2)}) %collective-permute-start.27) | collective-permute-done | bytes 16416 | tf_op jit(solution)/shard_map/ppermute | solution.py:24
  209.4 3.4 %collective-permute-done.29 = f32[1,4096]{1,0:T(1,128)S(1)} collective-permute-done((f32[1,4096]{1,0:T(1,128)S(1)}, f32[1,4096]{1,0:T(1,128)S(1)}, u32[]{:S(2)}, u32[]{:S(2)}) %collective-permute-start.29) | collective-permute-done | bytes 16416 | tf_op jit(solution)/shard_map/ppermute | solution.py:24
  222.4 3.4 %collective-permute-done.31 = f32[1,4096]{1,0:T(1,128)S(1)} collective-permute-done((f32[1,4096]{1,0:T(1,128)S(1)}, f32[1,4096]{1,0:T(1,128)S(1)}, u32[]{:S(2)}, u32[]{:S(2)}) %collective-permute-start.31) | collective-permute-done | bytes 16416 | tf_op jit(solution)/shard_map/ppermute | solution.py:24
  230.8 1.9 collective-permute-start.32
  235.1 3.4 %collective-permute-done.33 = f32[1,4096]{1,0:T(1,128)S(1)} collective-permute-done((f32[1,4096]{1,0:T(1,128)S(1)}, f32[1,4096]{1,0:T(1,128)S(1)}, u32[]{:S(2)}, u32[]{:S(2)}) %collective-permute-start.33) | collective-permute-done | bytes 16416 | tf_op jit(solution)/shard_map/ppermute | solution.py:24
  241.9 12.4 %all-gather.1 = f32[512,128]{1,0:T(8,128)S(1)} all-gather(f32[64,128]{1,0:T(8,128)S(1)} %bitcast_subtract_fusion), channel_id=3, replica_groups=mesh['tm'=8,'space'=4] {'tm'}, dimensions={0}, use_global_device_ids=true | all-gather | bytes 294912 | tf_op jit(solution)/shard_map/all_gather | solution.py:39
  (400 shorter events, 133.4 us)
Async XLA Ops:
  0.7 4.7 %collective-permute-start = (f32[64,128]{1,0:T(8,128)S(1)}, f32[64,128]{1,0:T(8,128)S(1)}, u32[]{:S(2)}, u32[]{:S(2)}) collective-permute-start(f32[64,128]{1,0:T(8,128)S(1)} %broadcast.14), channel_id=1, source_target_pairs={{0,4},{4,8},{8,12},{12,16},{16,20},{20,24},{24,28},{1,5},{5,9},{9,... | collective-permute-start | bytes 98312 | tf_op jit(solution)/shard_map/ppermute | solution.py:34
  9.0 6.6 %collective-permute-start.1 = (f32[1,4096]{1,0:T(1,128)S(1)}, f32[1,4096]{1,0:T(1,128)S(1)}, u32[]{:S(2)}, u32[]{:S(2)}) collective-permute-start(f32[1,4096]{1,0:T(1,128)S(1)} %stack_reshape.96), channel_id=1, source_target_pairs={{0,1},{1,2},{2,3},{4,5},{5,6},{6,7},{8,9},{9,10},{10,11},{12,13},{... | collective-permute-start | bytes 49160 | tf_op jit(solution)/shard_map/ppermute | solution.py:22
  14.2 5.8 %collective-permute-start.2 = (f32[1,4096]{1,0:T(1,128)S(1)}, f32[1,4096]{1,0:T(1,128)S(1)}, u32[]{:S(2)}, u32[]{:S(2)}) collective-permute-start(f32[1,4096]{1,0:T(1,128)S(1)} %stack_reshape.97), channel_id=1, source_target_pairs={{1,0},{2,1},{3,2},{5,4},{6,5},{7,6},{9,8},{10,9},{11,10},{13,12},{... | collective-permute-start | bytes 49160 | tf_op jit(solution)/shard_map/ppermute | solution.py:24
  24.9 5.1 %collective-permute-start.3 = (f32[1,4096]{1,0:T(1,128)S(1)}, f32[1,4096]{1,0:T(1,128)S(1)}, u32[]{:S(2)}, u32[]{:S(2)}) collective-permute-start(f32[1,4096]{1,0:T(1,128)S(1)} %stack_reshape.98), channel_id=1, source_target_pairs={{0,1},{1,2},{2,3},{4,5},{5,6},{6,7},{8,9},{9,10},{10,11},{12,13},{... | collective-permute-start | bytes 49160 | tf_op jit(solution)/shard_map/ppermute | solution.py:22
  28.6 5.6 %collective-permute-start.4 = (f32[1,4096]{1,0:T(1,128)S(1)}, f32[1,4096]{1,0:T(1,128)S(1)}, u32[]{:S(2)}, u32[]{:S(2)}) collective-permute-start(f32[1,4096]{1,0:T(1,128)S(1)} %stack_reshape.99), channel_id=1, source_target_pairs={{1,0},{2,1},{3,2},{5,4},{6,5},{7,6},{9,8},{10,9},{11,10},{13,12},{... | collective-permute-start | bytes 49160 | tf_op jit(solution)/shard_map/ppermute | solution.py:24
  39.6 5.1 %collective-permute-start.5 = (f32[1,4096]{1,0:T(1,128)S(1)}, f32[1,4096]{1,0:T(1,128)S(1)}, u32[]{:S(2)}, u32[]{:S(2)}) collective-permute-start(f32[1,4096]{1,0:T(1,128)S(1)} %stack_reshape.100), channel_id=1, source_target_pairs={{0,1},{1,2},{2,3},{4,5},{5,6},{6,7},{8,9},{9,10},{10,11},{12,13},{... | collective-permute-start | bytes 49160 | tf_op jit(solution)/shard_map/ppermute | solution.py:22
  43.3 5.6 %collective-permute-start.6 = (f32[1,4096]{1,0:T(1,128)S(1)}, f32[1,4096]{1,0:T(1,128)S(1)}, u32[]{:S(2)}, u32[]{:S(2)}) collective-permute-start(f32[1,4096]{1,0:T(1,128)S(1)} %stack_reshape.101), channel_id=1, source_target_pairs={{1,0},{2,1},{3,2},{5,4},{6,5},{7,6},{9,8},{10,9},{11,10},{13,12},{... | collective-permute-start | bytes 49160 | tf_op jit(solution)/shard_map/ppermute | solution.py:24
  53.8 3.5 %collective-permute-start.7 = (f32[1,4096]{1,0:T(1,128)S(1)}, f32[1,4096]{1,0:T(1,128)S(1)}, u32[]{:S(2)}, u32[]{:S(2)}) collective-permute-start(f32[1,4096]{1,0:T(1,128)S(1)} %stack_reshape.102), channel_id=1, source_target_pairs={{0,1},{1,2},{2,3},{4,5},{5,6},{6,7},{8,9},{9,10},{10,11},{12,13},{... | collective-permute-start | bytes 49160 | tf_op jit(solution)/shard_map/ppermute | solution.py:22
  56.0 5.6 %collective-permute-start.8 = (f32[1,4096]{1,0:T(1,128)S(1)}, f32[1,4096]{1,0:T(1,128)S(1)}, u32[]{:S(2)}, u32[]{:S(2)}) collective-permute-start(f32[1,4096]{1,0:T(1,128)S(1)} %stack_reshape.103), channel_id=1, source_target_pairs={{1,0},{2,1},{3,2},{5,4},{6,5},{7,6},{9,8},{10,9},{11,10},{13,12},{... | collective-permute-start | bytes 49160 | tf_op jit(solution)/shard_map/ppermute | solution.py:24
  66.9 3.5 %collective-permute-start.9 = (f32[1,4096]{1,0:T(1,128)S(1)}, f32[1,4096]{1,0:T(1,128)S(1)}, u32[]{:S(2)}, u32[]{:S(2)}) collective-permute-start(f32[1,4096]{1,0:T(1,128)S(1)} %stack_reshape.104), channel_id=1, source_target_pairs={{0,1},{1,2},{2,3},{4,5},{5,6},{6,7},{8,9},{9,10},{10,11},{12,13},{... | collective-permute-start | bytes 49160 | tf_op jit(solution)/shard_map/ppermute | solution.py:22
  69.1 5.6 %collective-permute-start.10 = (f32[1,4096]{1,0:T(1,128)S(1)}, f32[1,4096]{1,0:T(1,128)S(1)}, u32[]{:S(2)}, u32[]{:S(2)}) collective-permute-start(f32[1,4096]{1,0:T(1,128)S(1)} %stack_reshape.105), channel_id=1, source_target_pairs={{1,0},{2,1},{3,2},{5,4},{6,5},{7,6},{9,8},{10,9},{11,10},{13,12},{... | collective-permute-start | bytes 49160 | tf_op jit(solution)/shard_map/ppermute | solution.py:24
  79.6 3.5 %collective-permute-start.11 = (f32[1,4096]{1,0:T(1,128)S(1)}, f32[1,4096]{1,0:T(1,128)S(1)}, u32[]{:S(2)}, u32[]{:S(2)}) collective-permute-start(f32[1,4096]{1,0:T(1,128)S(1)} %stack_reshape.106), channel_id=1, source_target_pairs={{0,1},{1,2},{2,3},{4,5},{5,6},{6,7},{8,9},{9,10},{10,11},{12,13},{... | collective-permute-start | bytes 49160 | tf_op jit(solution)/shard_map/ppermute | solution.py:22
  81.8 5.6 %collective-permute-start.12 = (f32[1,4096]{1,0:T(1,128)S(1)}, f32[1,4096]{1,0:T(1,128)S(1)}, u32[]{:S(2)}, u32[]{:S(2)}) collective-permute-start(f32[1,4096]{1,0:T(1,128)S(1)} %stack_reshape.107), channel_id=1, source_target_pairs={{1,0},{2,1},{3,2},{5,4},{6,5},{7,6},{9,8},{10,9},{11,10},{13,12},{... | collective-permute-start | bytes 49160 | tf_op jit(solution)/shard_map/ppermute | solution.py:24
  92.6 3.7 %collective-permute-start.13 = (f32[1,4096]{1,0:T(1,128)S(1)}, f32[1,4096]{1,0:T(1,128)S(1)}, u32[]{:S(2)}, u32[]{:S(2)}) collective-permute-start(f32[1,4096]{1,0:T(1,128)S(1)} %stack_reshape.108), channel_id=1, source_target_pairs={{0,1},{1,2},{2,3},{4,5},{5,6},{6,7},{8,9},{9,10},{10,11},{12,13},{... | collective-permute-start | bytes 49160 | tf_op jit(solution)/shard_map/ppermute | solution.py:22
  94.8 5.6 %collective-permute-start.14 = (f32[1,4096]{1,0:T(1,128)S(1)}, f32[1,4096]{1,0:T(1,128)S(1)}, u32[]{:S(2)}, u32[]{:S(2)}) collective-permute-start(f32[1,4096]{1,0:T(1,128)S(1)} %stack_reshape.109), channel_id=1, source_target_pairs={{1,0},{2,1},{3,2},{5,4},{6,5},{7,6},{9,8},{10,9},{11,10},{13,12},{... | collective-permute-start | bytes 49160 | tf_op jit(solution)/shard_map/ppermute | solution.py:24
  105.4 15.0 %collective-permute-start.15 = (f32[1,4096]{1,0:T(1,128)S(1)}, f32[1,4096]{1,0:T(1,128)S(1)}, u32[]{:S(2)}, u32[]{:S(2)}) collective-permute-start(f32[1,4096]{1,0:T(1,128)S(1)} %stack_reshape.110), channel_id=1, source_target_pairs={{0,1},{1,2},{2,3},{4,5},{5,6},{6,7},{8,9},{9,10},{10,11},{12,13},{... | collective-permute-start | bytes 49160 | tf_op jit(solution)/shard_map/ppermute | solution.py:22
  107.5 13.7 %collective-permute-start.16 = (f32[1,4096]{1,0:T(1,128)S(1)}, f32[1,4096]{1,0:T(1,128)S(1)}, u32[]{:S(2)}, u32[]{:S(2)}) collective-permute-start(f32[1,4096]{1,0:T(1,128)S(1)} %stack_reshape.111), channel_id=1, source_target_pairs={{1,0},{2,1},{3,2},{5,4},{6,5},{7,6},{9,8},{10,9},{11,10},{13,12},{... | collective-permute-start | bytes 49160 | tf_op jit(solution)/shard_map/ppermute | solution.py:24
  138.1 6.1 %collective-permute-start.18 = (f32[1,4096]{1,0:T(1,128)S(1)}, f32[1,4096]{1,0:T(1,128)S(1)}, u32[]{:S(2)}, u32[]{:S(2)}) collective-permute-start(f32[1,4096]{1,0:T(1,128)S(1)} %stack_reshape.112), channel_id=1, source_target_pairs={{0,1},{1,2},{2,3},{4,5},{5,6},{6,7},{8,9},{9,10},{10,11},{12,13},{... | collective-permute-start | bytes 49160 | tf_op jit(solution)/shard_map/ppermute | solution.py:22
  142.9 5.7 %collective-permute-start.19 = (f32[1,4096]{1,0:T(1,128)S(1)}, f32[1,4096]{1,0:T(1,128)S(1)}, u32[]{:S(2)}, u32[]{:S(2)}) collective-permute-start(f32[1,4096]{1,0:T(1,128)S(1)} %stack_reshape.113), channel_id=1, source_target_pairs={{1,0},{2,1},{3,2},{5,4},{6,5},{7,6},{9,8},{10,9},{11,10},{13,12},{... | collective-permute-start | bytes 49160 | tf_op jit(solution)/shard_map/ppermute | solution.py:24
  153.5 3.4 %collective-permute-start.20 = (f32[1,4096]{1,0:T(1,128)S(1)}, f32[1,4096]{1,0:T(1,128)S(1)}, u32[]{:S(2)}, u32[]{:S(2)}) collective-permute-start(f32[1,4096]{1,0:T(1,128)S(1)} %stack_reshape.114), channel_id=1, source_target_pairs={{0,1},{1,2},{2,3},{4,5},{5,6},{6,7},{8,9},{9,10},{10,11},{12,13},{... | collective-permute-start | bytes 49160 | tf_op jit(solution)/shard_map/ppermute | solution.py:22
  155.6 5.6 %collective-permute-start.21 = (f32[1,4096]{1,0:T(1,128)S(1)}, f32[1,4096]{1,0:T(1,128)S(1)}, u32[]{:S(2)}, u32[]{:S(2)}) collective-permute-start(f32[1,4096]{1,0:T(1,128)S(1)} %stack_reshape.115), channel_id=1, source_target_pairs={{1,0},{2,1},{3,2},{5,4},{6,5},{7,6},{9,8},{10,9},{11,10},{13,12},{... | collective-permute-start | bytes 49160 | tf_op jit(solution)/shard_map/ppermute | solution.py:24
  166.5 3.5 %collective-permute-start.22 = (f32[1,4096]{1,0:T(1,128)S(1)}, f32[1,4096]{1,0:T(1,128)S(1)}, u32[]{:S(2)}, u32[]{:S(2)}) collective-permute-start(f32[1,4096]{1,0:T(1,128)S(1)} %stack_reshape.116), channel_id=1, source_target_pairs={{0,1},{1,2},{2,3},{4,5},{5,6},{6,7},{8,9},{9,10},{10,11},{12,13},{... | collective-permute-start | bytes 49160 | tf_op jit(solution)/shard_map/ppermute | solution.py:22
  168.7 5.6 %collective-permute-start.23 = (f32[1,4096]{1,0:T(1,128)S(1)}, f32[1,4096]{1,0:T(1,128)S(1)}, u32[]{:S(2)}, u32[]{:S(2)}) collective-permute-start(f32[1,4096]{1,0:T(1,128)S(1)} %stack_reshape.117), channel_id=1, source_target_pairs={{1,0},{2,1},{3,2},{5,4},{6,5},{7,6},{9,8},{10,9},{11,10},{13,12},{... | collective-permute-start | bytes 49160 | tf_op jit(solution)/shard_map/ppermute | solution.py:24
  179.2 3.5 %collective-permute-start.24 = (f32[1,4096]{1,0:T(1,128)S(1)}, f32[1,4096]{1,0:T(1,128)S(1)}, u32[]{:S(2)}, u32[]{:S(2)}) collective-permute-start(f32[1,4096]{1,0:T(1,128)S(1)} %stack_reshape.118), channel_id=1, source_target_pairs={{0,1},{1,2},{2,3},{4,5},{5,6},{6,7},{8,9},{9,10},{10,11},{12,13},{... | collective-permute-start | bytes 49160 | tf_op jit(solution)/shard_map/ppermute | solution.py:22
  181.4 5.6 %collective-permute-start.25 = (f32[1,4096]{1,0:T(1,128)S(1)}, f32[1,4096]{1,0:T(1,128)S(1)}, u32[]{:S(2)}, u32[]{:S(2)}) collective-permute-start(f32[1,4096]{1,0:T(1,128)S(1)} %stack_reshape.119), channel_id=1, source_target_pairs={{1,0},{2,1},{3,2},{5,4},{6,5},{7,6},{9,8},{10,9},{11,10},{13,12},{... | collective-permute-start | bytes 49160 | tf_op jit(solution)/shard_map/ppermute | solution.py:24
  192.3 3.7 %collective-permute-start.26 = (f32[1,4096]{1,0:T(1,128)S(1)}, f32[1,4096]{1,0:T(1,128)S(1)}, u32[]{:S(2)}, u32[]{:S(2)}) collective-permute-start(f32[1,4096]{1,0:T(1,128)S(1)} %stack_reshape.120), channel_id=1, source_target_pairs={{0,1},{1,2},{2,3},{4,5},{5,6},{6,7},{8,9},{9,10},{10,11},{12,13},{... | collective-permute-start | bytes 49160 | tf_op jit(solution)/shard_map/ppermute | solution.py:22
  194.5 5.6 %collective-permute-start.27 = (f32[1,4096]{1,0:T(1,128)S(1)}, f32[1,4096]{1,0:T(1,128)S(1)}, u32[]{:S(2)}, u32[]{:S(2)}) collective-permute-start(f32[1,4096]{1,0:T(1,128)S(1)} %stack_reshape.121), channel_id=1, source_target_pairs={{1,0},{2,1},{3,2},{5,4},{6,5},{7,6},{9,8},{10,9},{11,10},{13,12},{... | collective-permute-start | bytes 49160 | tf_op jit(solution)/shard_map/ppermute | solution.py:24
  205.0 3.5 %collective-permute-start.28 = (f32[1,4096]{1,0:T(1,128)S(1)}, f32[1,4096]{1,0:T(1,128)S(1)}, u32[]{:S(2)}, u32[]{:S(2)}) collective-permute-start(f32[1,4096]{1,0:T(1,128)S(1)} %stack_reshape.122), channel_id=1, source_target_pairs={{0,1},{1,2},{2,3},{4,5},{5,6},{6,7},{8,9},{9,10},{10,11},{12,13},{... | collective-permute-start | bytes 49160 | tf_op jit(solution)/shard_map/ppermute | solution.py:22
  207.2 5.6 %collective-permute-start.29 = (f32[1,4096]{1,0:T(1,128)S(1)}, f32[1,4096]{1,0:T(1,128)S(1)}, u32[]{:S(2)}, u32[]{:S(2)}) collective-permute-start(f32[1,4096]{1,0:T(1,128)S(1)} %stack_reshape.123), channel_id=1, source_target_pairs={{1,0},{2,1},{3,2},{5,4},{6,5},{7,6},{9,8},{10,9},{11,10},{13,12},{... | collective-permute-start | bytes 49160 | tf_op jit(solution)/shard_map/ppermute | solution.py:24
  218.0 3.5 %collective-permute-start.30 = (f32[1,4096]{1,0:T(1,128)S(1)}, f32[1,4096]{1,0:T(1,128)S(1)}, u32[]{:S(2)}, u32[]{:S(2)}) collective-permute-start(f32[1,4096]{1,0:T(1,128)S(1)} %stack_reshape.124), channel_id=1, source_target_pairs={{0,1},{1,2},{2,3},{4,5},{5,6},{6,7},{8,9},{9,10},{10,11},{12,13},{... | collective-permute-start | bytes 49160 | tf_op jit(solution)/shard_map/ppermute | solution.py:22
  220.2 5.6 %collective-permute-start.31 = (f32[1,4096]{1,0:T(1,128)S(1)}, f32[1,4096]{1,0:T(1,128)S(1)}, u32[]{:S(2)}, u32[]{:S(2)}) collective-permute-start(f32[1,4096]{1,0:T(1,128)S(1)} %stack_reshape.125), channel_id=1, source_target_pairs={{1,0},{2,1},{3,2},{5,4},{6,5},{7,6},{9,8},{10,9},{11,10},{13,12},{... | collective-permute-start | bytes 49160 | tf_op jit(solution)/shard_map/ppermute | solution.py:24
  232.9 5.6 %collective-permute-start.33 = (f32[1,4096]{1,0:T(1,128)S(1)}, f32[1,4096]{1,0:T(1,128)S(1)}, u32[]{:S(2)}, u32[]{:S(2)}) collective-permute-start(f32[1,4096]{1,0:T(1,128)S(1)} %stack_reshape.127), channel_id=1, source_target_pairs={{1,0},{2,1},{3,2},{5,4},{6,5},{7,6},{9,8},{10,9},{11,10},{13,12},{... | collective-permute-start | bytes 49160 | tf_op jit(solution)/shard_map/ppermute | solution.py:24
  (8 other events, 69.7 us)
where the time goes:
time: 256 us; the launch traced here: 255 us
  starting transfers between devices  64.8 us (25%)
  local copies, waits for them, and re-layouts  59.2 us (23%)
  waiting for transfers between devices  51.5 us (20%)
  other arithmetic  39.1 us (15%)
  blocking collectives  32.3 us (13%)
  matrix products  5.41 us (2%)
  between operations  2.56 us (1%)
    ppermute x16, waiting for transfers between devices, extended_2(): lax.ppermute(head, axis, [((i + 1) % count, i) for i in range(ends)])  50.6 us
    ppermute x16, starting transfers between devices, extended_2(): lax.ppermute(tail, axis, [(i, (i + 1) % count) for i in range(ends)])  38.8 us
    all_gather x3, blocking collectives, carried_in(): gathered = jax.tree.map(lambda a: lax.all_gather(a, axis), part)  32.3 us
    gather x32, local copies, waits for them, and re-layouts, coupling(): jnp.take(extended, jnp.maximum(neighbor, 0), axis=1) * face_valid[None]  27.5 us
    ppermute x16, starting transfers between devices, extended_2(): lax.ppermute(head, axis, [((i + 1) % count, i) for i in range(ends)])  21.2 us
    ppermute x16, other arithmetic, extended_2(): lax.ppermute(tail, axis, [(i, (i + 1) % count) for i in range(ends)])  11.6 us
    ppermute x16, other arithmetic, extended_2(): lax.ppermute(head, axis, [((i + 1) % count, i) for i in range(ends)])  11.6 us
    gather x16, local copies, waits for them, and re-layouts, extend(): upper_rows = jnp.take(field_now, send_rows[1], axis=1)  9.65 us
  transfers between devices with their start and end apart: 34, of which 16 were waited for; matrix products, arithmetic and copies ran while one was open for 8% of the time, Pallas kernels for 0%

commit v1 on v0

v1 whole, which is shorter than its diff:
```python
import functools

import jax
import jax.numpy as jnp
from jax import lax
from jax.experimental import pallas as pl
from jax.experimental.pallas import tpu as pltpu
from jax.sharding import PartitionSpec as P

SWEEPS = 2
ITERS = 2
LANES = 128
SUB = 8
MESH = pl.DeviceIdType.MESH


def pick(block, index):
    return jnp.concatenate(
        [
            jnp.take_along_axis(block[r : r + SUB], index, axis=1, mode="promise_in_bounds")
            for r in range(0, block.shape[0], SUB)
        ],
        axis=0,
    )


def masked(value, mask):
    return jnp.concatenate(
        [jnp.where(mask, value[r : r + SUB], 0.0) for r in range(0, value.shape[0], SUB)], axis=0
    )


def kernel(
    tm, ns, steps,
    init_ref, forcing_ref, gain_ref, inverse_ref, faces_ref, neighbor_ref, send_rows_ref,
    coarse_ref, residual_ref,
    inv_t, wide, f_ref, r_ref, idx_ref,
    send_up, send_dn, below, above,
    gbuf, rbuf, cbuf, cin,
    up_send, up_recv, dn_send, dn_recv,
    g_send, g_recv, a_send, a_recv, c_send, c_recv,
):
    values, elems = init_ref.shape
    layer = elems // 2
    half = values // 2
    scanners = min(tm, values // SUB)
    rows = values // scanners
    k = lax.axis_index("tm")
    p = lax.axis_index("space")

    barrier = pltpu.get_barrier_semaphore()
    for d in range(1, tm):
        pl.semaphore_signal(barrier, inc=1, device_id=(lax.rem(k + d, tm), p), device_id_type=MESH)

    @pl.when(p > 0)
    def _():
        pl.semaphore_signal(barrier, inc=1, device_id=(k, p - 1), device_id_type=MESH)

    @pl.when(p < ns - 1)
    def _():
        pl.semaphore_signal(barrier, inc=1, device_id=(k, p + 1), device_id_type=MESH)

    def turn(j, carry):
        for i in range(0, values, SUB):
            inv_t[j, pl.ds(i, SUB), :] = inverse_ref[pl.ds(i * values + j, SUB, stride=values), :]
        return carry

    lax.fori_loop(0, values, turn, 0, unroll=4)

    for f in range(6):
        part = faces_ref[(4, 5, 0, 1, 2, 3)[f]]
        high = part.astype(jnp.bfloat16).astype(jnp.float32)
        low = part - high
        for c, piece in enumerate((high, low, high, low)):
            wide[f * values : (f + 1) * values, c * values : (c + 1) * values] = piece
    f_ref[...] = wide[...].astype(jnp.bfloat16)

    for row in range(2):
        for at in (0, layer):
            idx_ref[row : row + 1, at : at + layer] = send_rows_ref[row : row + 1, :]

    def spread(row):
        return jnp.broadcast_to(row, (SUB, LANES))

    low_index = spread(idx_ref[0:1, :])
    high_index = spread(idx_ref[1:2, :])
    lane = lax.broadcasted_iota(jnp.int32, (SUB, LANES), 1)
    first_half = lane < layer
    side = [spread(neighbor_ref[f : f + 1, :]) for f in range(6)]
    own_mask = [(n >= 0) & (n < elems) for n in side]
    own_index = [jnp.clip(n, 0, elems - 1) for n in side]
    halo_mask, halo_index = [], []
    for n, base in ((side[4], elems), (side[5], elems + layer)):
        halo_mask.append((n >= base) & (n < base + layer))
        halo_index.append(jnp.clip(n - base, 0, layer - 1))

    @pl.when(p == 0)
    def _():
        below[...] = jnp.zeros_like(below)

    @pl.when(p == ns - 1)
    def _():
        above[...] = jnp.zeros_like(above)

    expected = tm - 1 + (p > 0).astype(jnp.int32) + (p < ns - 1).astype(jnp.int32)
    pl.semaphore_wait(barrier, expected)

    def when_scanner(place, run):
        if scanners == tm:
            run()
        else:
            pl.when(place < scanners)(run)

    def to_scanner(src, dst, d, send, recv):
        place = lax.rem(k + d, tm)
        return pltpu.make_async_remote_copy(
            src_ref=src.at[pl.ds(pl.multiple_of(lax.rem(place, scanners) * rows, SUB), rows)],
            dst_ref=dst.at[k], send_sem=send.at[d], recv_sem=recv.at[d],
            device_id=(place, p), device_id_type=MESH,
        )

    def from_scanner(d):
        place = lax.rem(k + d, tm)
        return pltpu.make_async_remote_copy(
            src_ref=cbuf.at[place],
            dst_ref=cin.at[pl.ds(pl.multiple_of(lax.rem(k, scanners) * rows, SUB), rows)],
            send_sem=c_send.at[d], recv_sem=c_recv.at[d],
            device_id=(place, p), device_id_type=MESH,
        )

    my_rows = pl.ds(pl.multiple_of(lax.rem(k, scanners) * rows, SUB), rows)
    gains = gain_ref.at[0]
    for d in range(1, tm):
        when_scanner(lax.rem(k + d, tm), lambda d=d: to_scanner(gains, gbuf, d, g_send, g_recv).start())

    def apply_inverse(vector):
        r_ref[...] = vector
        sums = [None, None]
        for j in range(values):
            term = inv_t[j] * r_ref[j : j + 1, :]
            sums[j % 2] = term if sums[j % 2] is None else sums[j % 2] + term
        return sums[0] + sums[1]

    def up_copy(s):
        return pltpu.make_async_remote_copy(
            src_ref=send_up.at[s], dst_ref=below.at[s], send_sem=up_send.at[s],
            recv_sem=up_recv.at[s], device_id=(k, p + 1), device_id_type=MESH,
        )

    def dn_copy(s):
        return pltpu.make_async_remote_copy(
            src_ref=send_dn.at[s], dst_ref=above.at[s], send_sem=dn_send.at[s],
            recv_sem=dn_recv.at[s], device_id=(k, p - 1), device_id_type=MESH,
        )

    def packed(block, index):
        halves = [pick(block[:half], index), pick(block[half:], index)]
        return jnp.concatenate(
            [
                jnp.where(first_half, halves[0][r : r + SUB], halves[1][r : r + SUB])
                for r in range(0, half, SUB)
            ],
            axis=0,
        )

    def unpacked(block, index, mask):
        return masked(
            jnp.concatenate([pick(block, index), pick(block, index + layer)], axis=0), mask
        )

    def remainder(x, b, s):
        high = x.astype(jnp.bfloat16)
        low = (x - high.astype(jnp.float32)).astype(jnp.bfloat16)
        stack = jnp.concatenate([high, high, low, low], axis=0)
        along_z = jnp.dot(
            f_ref[: 2 * values, :], stack, preferred_element_type=jnp.float32
        )
        minus_z, plus_z = along_z[:values], along_z[values:]
        send_up[s] = packed(minus_z, high_index)
        send_dn[s] = packed(plus_z, low_index)

        @pl.when(p < ns - 1)
        def _():
            up_copy(s).start()

        @pl.when(p > 0)
        def _():
            dn_copy(s).start()

        along_xy = jnp.dot(
            f_ref[2 * values :, :], stack, preferred_element_type=jnp.float32
        )
        rest = b - masked(pick(minus_z, own_index[4]), own_mask[4])
        rest = rest - masked(pick(plus_z, own_index[5]), own_mask[5])
        for f in range(4):
            product = along_xy[f * values : (f + 1) * values]
            rest = rest - masked(pick(product, own_index[f]), own_mask[f])

        @pl.when(p < ns - 1)
        def _():
            up_copy(s).wait_send()
            dn_copy(s).wait_recv()

        @pl.when(p > 0)
        def _():
            dn_copy(s).wait_send()
            up_copy(s).wait_recv()

        rest = rest - unpacked(below[s], halo_index[0], halo_mask[0])
        return rest - unpacked(above[s], halo_index[1], halo_mask[1])

    def fine_step(m, field):
        b = field + forcing_ref[m]
        x = apply_inverse(b)
        for sweep in range(SWEEPS):
            x = apply_inverse(remainder(x, b, sweep % 2))
        return x

    def carried_in(first):
        res = residual_ref.at[0]
        for d in range(1, tm):
            when_scanner(
                lax.rem(k + d, tm), lambda d=d: to_scanner(res, rbuf, d, a_send, a_recv).start()
            )

        def scan():
            rbuf[k] = res[my_rows, :]
            if first:
                gbuf[k] = gains[my_rows, :]
                for d in range(1, tm):
                    to_scanner(gains, gbuf, d, g_send, g_recv).wait_recv()
            for d in range(1, tm):
                to_scanner(res, rbuf, d, a_send, a_recv).wait_recv()
            running = jnp.zeros((rows, LANES), jnp.float32)
            for lap in range(tm):
                cbuf[lap] = running
                running = gbuf[lap] * running + rbuf[lap]
            for d in range(1, tm):
                from_scanner(d).start()
            cin[my_rows, :] = cbuf[k]

        when_scanner(k, scan)
        for d in range(1, tm):

            def sent(d=d):
                if first:
                    to_scanner(gains, gbuf, d, g_send, g_recv).wait_send()
                to_scanner(res, rbuf, d, a_send, a_recv).wait_send()

            when_scanner(lax.rem(k + d, tm), sent)
            when_scanner(lax.rem(k + tm - d, tm), lambda d=d: from_scanner(d).wait_recv())

        def returned():
            for d in range(1, tm):
                from_scanner(d).wait_send()

        when_scanner(k, returned)
        return cin[...]

    coarse = jnp.zeros((values, elems), jnp.float32)
    previous = coarse
    for iteration in range(ITERS):
        field = lax.fori_loop(
            0, steps, fine_step, jnp.where(k == 0, init_ref[...], previous)
        )
        residual = field - coarse
        residual_ref[0] = residual
        carried = carried_in(iteration == 0)
        previous = previous + carried
        coarse = coarse + (gain_ref[0] * carried + residual)
    coarse_ref[0] = coarse


def body(tm, ns, initial_state, forcing, coarse_gain, block_inverse, face_blocks, neighbor, send_rows):
    values, elems = initial_state.shape
    steps = forcing.shape[0]
    scanners = min(tm, values // SUB)
    rows = values // scanners
    f32 = jnp.float32
    out = jax.ShapeDtypeStruct((1, values, elems), f32)
    vmem = pl.BlockSpec(memory_space=pltpu.VMEM)
    dma = pltpu.SemaphoreType.DMA
    return tuple(
        pl.pallas_call(
            functools.partial(kernel, tm, ns, steps),
            out_shape=(out, out),
            in_specs=[vmem] * 7,
            out_specs=(vmem, vmem),
            scratch_shapes=[
                pltpu.VMEM((values, values, elems), f32),
                pltpu.VMEM((6 * values, 4 * values), f32),
                pltpu.VMEM((6 * values, 4 * values), jnp.bfloat16),
                pltpu.VMEM((values, elems), f32),
                pltpu.VMEM((SUB, elems), jnp.int32),
                pltpu.VMEM((2, values // 2, elems), f32),
                pltpu.VMEM((2, values // 2, elems), f32),
                pltpu.VMEM((2, values // 2, elems), f32),
                pltpu.VMEM((2, values // 2, elems), f32),
                pltpu.VMEM((tm, rows, elems), f32),
                pltpu.VMEM((tm, rows, elems), f32),
                pltpu.VMEM((tm, rows, elems), f32),
                pltpu.VMEM((values, elems), f32),
                dma((2,)), dma((2,)), dma((2,)), dma((2,)),
                dma((tm,)), dma((tm,)), dma((tm,)), dma((tm,)), dma((tm,)), dma((tm,)),
            ],
            compiler_params=pltpu.CompilerParams(
                collective_id=0, has_side_effects=True, vmem_limit_bytes=32 * 1024 * 1024
            ),
        )(
            initial_state, forcing, coarse_gain,
            block_inverse.reshape(values * values, elems), face_blocks, neighbor, send_rows,
        )
    )


def solution(mesh):
    return jax.shard_map(
        functools.partial(body, mesh.shape["tm"], mesh.shape["space"]),
        mesh=mesh,
        in_specs=(
            P(None, "space"),
            P("tm", None, "space"),
            P("tm", None, "space"),
            P(None, None, "space"),
            P(),
            P(None, "space"),
            P(None, "space"),
        ),
        out_specs=(P("tm", None, "space"), P("tm", None, "space")),
        check_vma=False,
    )
```

time: 256 us -> 79.1 us (0.31)
  Pallas kernels: 0 us -> 70.5 us
  starting transfers between devices: 64.8 us -> 0 us
  local copies, waits for them, and re-layouts: 59.2 us -> 7.53 us
  waiting for transfers between devices: 51.5 us -> 0 us
  other arithmetic: 39.1 us -> 0 us
  blocking collectives: 32.3 us -> 0 us
  matrix products: 5.41 us -> 0 us
    pallas_call x0 -> x1, Pallas kernels: none -> 70.5 us  [body(): pl.pallas_call(functools.partial(kernel, tm, ns, steps), out_shape=(out,...]
    ppermute x34 -> x0, starting transfers between devices: 64.8 us -> none  [the longest x16 38.8 us: extended_2(): lax.ppermute(tail, axis, [(i, (i + 1) % count) for i in range(ends)])]
    ppermute x34 -> x0, waiting for transfers between devices: 51.5 us -> none  [the longest x16 50.6 us: extended_2(): lax.ppermute(head, axis, [((i + 1) % count, i) for i in range(ends)])]
    gather x64 -> x0, local copies, waits for them, and re-layouts: 46.7 us -> none  [the longest x32 27.5 us: coupling(): jnp.take(extended, jnp.maximum(neighbor, 0), axis=1) * face_valid[None]]
    all_gather x3 -> x0, blocking collectives: 32.3 us -> none  [carried_in(): gathered = jax.tree.map(lambda a: lax.all_gather(a, axis), part)]
    ppermute x32 -> x0, other arithmetic: 23.3 us -> none  [the longest x16 11.6 us: extended_2(): lax.ppermute(tail, axis, [(i, (i + 1) % count) for i in range(ends)])]
    another operation x98 -> x0, local copies, waits for them, and re-layouts: 7.9 us -> none  [the longest x32 3.16 us: extend(): stacked = jnp.stack([bottom.reshape(-1), upper_rows.reshape(-1)], axis=0)]
    unnamed x12 -> x16, local copies, waits for them, and re-layouts: 0.09 us -> 7.53 us
  transfers between devices with their start and end apart: 34 -> 0, of which waited for: 16 -> 0; matrix products, arithmetic and copies ran while one was open for 8% -> 0% of each run, Pallas kernels for 0% -> 0%
where the time goes in v1:
time: 79.1 us; the launch traced here: 78.7 us
  Pallas kernels  70.5 us (89%)
  local copies, waits for them, and re-layouts  7.53 us (10%)
    pallas_call x1, Pallas kernels, body(): pl.pallas_call(functools.partial(kernel, tm, ns, steps), out_shape=(out,...  70.5 us
    unnamed x16, local copies, waits for them, and re-layouts  7.53 us

profile of v1, /device:TPU:0, one launch (start us, length us, event | category | flops | bytes accessed | tf_op | source)
XLA Modules:
  0.0 78.7 jit_solution(17731500234864112914)
XLA Ops:
  0.6 0.0 copy-start
  0.6 1.6 %copy-done = f32[64,64,128]{2,1,0:T(8,128)S(1)} copy-done((f32[64,64,128]{2,1,0:T(8,128)S(1)}, f32[64,64,128]{2,1,0:T(8,128)}, u32[]{:S(2)}) %copy-start) | copy-done | bytes 2097176
  2.2 0.0 copy-start.1
  2.2 0.9 %copy-done.1 = f32[6,64,64]{2,1,0:T(8,128)S(1)} copy-done((f32[6,64,64]{2,1,0:T(8,128)S(1)}, f32[6,64,64]{2,1,0:T(8,128)}, u32[]{:S(2)}) %copy-start.1) | copy-done | bytes 98328
  3.2 0.0 copy-start.2
  3.2 0.9 %copy-done.2 = f32[4,64,128]{2,1,0:T(8,128)S(1)} copy-done((f32[4,64,128]{2,1,0:T(8,128)S(1)}, f32[4,64,128]{2,1,0:T(8,128)}, u32[]{:S(2)}) %copy-start.2) | copy-done | bytes 131096
  4.1 0.0 copy-start.3
  4.1 0.8 copy-done.3
  4.8 0.0 copy-start.4
  4.8 0.8 copy-done.4
  5.6 0.0 copy-start.5
  5.6 0.7 copy-done.5
  6.3 0.0 copy-start.6
  6.3 0.7 copy-done.6
  6.9 70.5 %shard_map.86 = (f32[1,64,128]{2,1,0:T(8,128)S(1)}, f32[1,64,128]{2,1,0:T(8,128)S(1)}) custom-call(f32[64,128]{1,0:T(8,128)S(1)} %copy-done.3, f32[4,64,128]{2,1,0:T(8,128)S(1)} %copy-done.2, f32[1,64,128]{2,1,0:T(8,128)S(1)} %copy-done.4, f32[4096,128]{1,0:T(8,128)S(1)} %bitcast.1, f32[6,64,64]{2,1,0:T(8,128)S(1)} %copy-done.1, s32[6,128]{1,0:T(8,128)S(1)} %copy-done.5, ...), custom_call_target="tpu_custom_call" | custom-call | tf_op jit(solution)/shard_map/pallas_call | solution.py:284
  77.5 0.6 copy.11
  78.1 0.6 copy.12
Async XLA Ops:
  0.6 1.6 %copy-start = (f32[64,64,128]{2,1,0:T(8,128)S(1)}, f32[64,64,128]{2,1,0:T(8,128)}, u32[]{:S(2)}) copy-start(f32[64,64,128]{2,1,0:T(8,128)} %param.10) | copy-start | bytes 6291460
  2.2 0.9 %copy-start.1 = (f32[6,64,64]{2,1,0:T(8,128)S(1)}, f32[6,64,64]{2,1,0:T(8,128)}, u32[]{:S(2)}) copy-start(f32[6,64,64]{2,1,0:T(8,128)} %faces_ref.1) | copy-start | bytes 294916
  3.2 0.9 %copy-start.2 = (f32[4,64,128]{2,1,0:T(8,128)S(1)}, f32[4,64,128]{2,1,0:T(8,128)}, u32[]{:S(2)}) copy-start(f32[4,64,128]{2,1,0:T(8,128)} %forcing_ref.1) | copy-start | bytes 393220
  4.1 0.8 copy-start.3
  4.8 0.8 copy-start.4
  5.6 0.7 copy-start.5
  6.3 0.7 copy-start.6

commit v2 on v1

--- a/solution.py
+++ b/solution.py
@@ -32,8 +32,10 @@
 
 def kernel(
     tm, ns, steps,
+    init_hbm, forcing_hbm, gain_hbm, inverse_hbm, faces_hbm, neighbor_hbm, send_rows_hbm,
+    out_ref,
     init_ref, forcing_ref, gain_ref, inverse_ref, faces_ref, neighbor_ref, send_rows_ref,
-    coarse_ref, residual_ref,
+    load_sem, res,
     inv_t, wide, f_ref, r_ref, idx_ref,
     send_up, send_dn, below, above,
     gbuf, rbuf, cbuf, cin,
@@ -48,6 +50,23 @@
     k = lax.axis_index("tm")
     p = lax.axis_index("space")
 
+    loads = [
+        pltpu.make_async_copy(src, dst, load_sem.at[n])
+        for n, (src, dst) in enumerate(
+            (
+                (inverse_hbm, inverse_ref),
+                (faces_hbm, faces_ref),
+                (neighbor_hbm, neighbor_ref),
+                (send_rows_hbm, send_rows_ref),
+                (init_hbm, init_ref),
+                (forcing_hbm, forcing_ref),
+                (gain_hbm, gain_ref),
+            )
+        )
+    ]
+    for load in loads:
+        load.start()
+
     barrier = pltpu.get_barrier_semaphore()
     for d in range(1, tm):
         pl.semaphore_signal(barrier, inc=1, device_id=(lax.rem(k + d, tm), p), device_id_type=MESH)
@@ -60,12 +79,8 @@
     def _():
         pl.semaphore_signal(barrier, inc=1, device_id=(k, p + 1), device_id_type=MESH)
 
-    def turn(j, carry):
-        for i in range(0, values, SUB):
-            inv_t[j, pl.ds(i, SUB), :] = inverse_ref[pl.ds(i * values + j, SUB, stride=values), :]
-        return carry
-
-    lax.fori_loop(0, values, turn, 0, unroll=4)
+    for load in loads[1:]:
+        load.wait()
 
     for f in range(6):
         part = faces_ref[(4, 5, 0, 1, 2, 3)[f]]
@@ -102,6 +117,15 @@
     def _():
         above[...] = jnp.zeros_like(above)
 
+    loads[0].wait()
+
+    def turn(j, carry):
+        for i in range(0, values, SUB):
+            inv_t[j, pl.ds(i, SUB), :] = inverse_ref[pl.ds(i * values + j, SUB, stride=values), :]
+        return carry
+
+    lax.fori_loop(0, values, turn, 0, unroll=4)
+
     expected = tm - 1 + (p > 0).astype(jnp.int32) + (p < ns - 1).astype(jnp.int32)
     pl.semaphore_wait(barrier, expected)
 
@@ -168,6 +192,15 @@
             jnp.concatenate([pick(block, index), pick(block, index + layer)], axis=0), mask
         )
 
+    def sent_halo(s, also):
+        @pl.when((p < ns - 1) & also)
+        def _():
+            up_copy(s).wait_send()
+
+        @pl.when((p > 0) & also)
+        def _():
+            dn_copy(s).wait_send()
+
     def remainder(x, b, s):
         high = x.astype(jnp.bfloat16)
         low = (x - high.astype(jnp.float32)).astype(jnp.bfloat16)
@@ -198,12 +231,10 @@
 
         @pl.when(p < ns - 1)
         def _():
-            up_copy(s).wait_send()
             dn_copy(s).wait_recv()
 
         @pl.when(p > 0)
         def _():
-            dn_copy(s).wait_send()
             up_copy(s).wait_recv()
 
         rest = rest - unpacked(below[s], halo_index[0], halo_mask[0])
@@ -213,11 +244,15 @@
         b = field + forcing_ref[m]
         x = apply_inverse(b)
         for sweep in range(SWEEPS):
-            x = apply_inverse(remainder(x, b, sweep % 2))
+            rest = remainder(x, b, sweep)
+            if sweep == 0:
+                sent_halo(SWEEPS - 1, m > 0)
+            else:
+                sent_halo(sweep - 1, True)
+            x = apply_inverse(rest)
         return x
 
     def carried_in(first):
-        res = residual_ref.at[0]
         for d in range(1, tm):
             when_scanner(
                 lax.rem(k + d, tm), lambda d=d: to_scanner(res, rbuf, d, a_send, a_recv).start()
@@ -263,12 +298,14 @@
         field = lax.fori_loop(
             0, steps, fine_step, jnp.where(k == 0, init_ref[...], previous)
         )
+        sent_halo(SWEEPS - 1, True)
         residual = field - coarse
-        residual_ref[0] = residual
+        res[...] = residual
         carried = carried_in(iteration == 0)
         previous = previous + carried
         coarse = coarse + (gain_ref[0] * carried + residual)
-    coarse_ref[0] = coarse
+    out_ref[0] = coarse
+    out_ref[1] = residual
 
 
 def body(tm, ns, initial_state, forcing, coarse_gain, block_inverse, face_blocks, neighbor, send_rows):
@@ -277,16 +314,25 @@
     scanners = min(tm, values // SUB)
     rows = values // scanners
     f32 = jnp.float32
-    out = jax.ShapeDtypeStruct((1, values, elems), f32)
+    out = jax.ShapeDtypeStruct((2, values, elems), f32)
     vmem = pl.BlockSpec(memory_space=pltpu.VMEM)
     dma = pltpu.SemaphoreType.DMA
-    return tuple(
+    both = (
         pl.pallas_call(
             functools.partial(kernel, tm, ns, steps),
-            out_shape=(out, out),
-            in_specs=[vmem] * 7,
-            out_specs=(vmem, vmem),
+            out_shape=out,
+            in_specs=[pl.BlockSpec(memory_space=pl.ANY)] * 7,
+            out_specs=vmem,
             scratch_shapes=[
+                pltpu.VMEM((values, elems), f32),
+                pltpu.VMEM(forcing.shape, f32),
+                pltpu.VMEM((1, values, elems), f32),
+                pltpu.VMEM((values * values, elems), f32),
+                pltpu.VMEM(face_blocks.shape, f32),
+                pltpu.VMEM(neighbor.shape, jnp.int32),
+                pltpu.VMEM(send_rows.shape, jnp.int32),
+                dma((7,)),
+                pltpu.VMEM((values, elems), f32),
                 pltpu.VMEM((values, values, elems), f32),
                 pltpu.VMEM((6 * values, 4 * values), f32),
                 pltpu.VMEM((6 * values, 4 * values), jnp.bfloat16),
@@ -304,13 +350,14 @@
                 dma((tm,)), dma((tm,)), dma((tm,)), dma((tm,)), dma((tm,)), dma((tm,)),
             ],
             compiler_params=pltpu.CompilerParams(
-                collective_id=0, has_side_effects=True, vmem_limit_bytes=32 * 1024 * 1024
+                collective_id=0, has_side_effects=True, vmem_limit_bytes=63 * 1024 * 1024
             ),
         )(
             initial_state, forcing, coarse_gain,
             block_inverse.reshape(values * values, elems), face_blocks, neighbor, send_rows,
         )
     )
+    return both[:1], both[1:]
 
 
 def solution(mesh):

time: 79.1 us -> 75.2 us (0.951)
  local copies, waits for them, and re-layouts: 7.53 us -> 1.4 us
  Pallas kernels: 70.5 us -> 72.9 us
    unnamed x16 -> x0, local copies, waits for them, and re-layouts: 7.53 us -> none
    pallas_call x1, Pallas kernels: 70.5 us -> 72.9 us  [body(): pl.pallas_call(functools.partial(kernel, tm, ns, steps), out_shape=out, i...]
    slice x0 -> x1, local copies, waits for them, and re-layouts: none -> 1.4 us  [body(): return (both[:1], both[1:])]
where the time goes in v2:
time: 75.2 us; the launch traced here: 74.9 us
  Pallas kernels  72.9 us (97%)
  local copies, waits for them, and re-layouts  1.4 us (2%)
    pallas_call x1, Pallas kernels, body(): pl.pallas_call(functools.partial(kernel, tm, ns, steps), out_shape=out, i...  72.9 us

profile of v2, /device:TPU:0, one launch (start us, length us, event | category | flops | bytes accessed | tf_op | source)
XLA Modules:
  0.0 74.9 jit_solution(18016408433237005236)
XLA Ops:
  0.6 72.9 %shard_map.86 = f32[2,64,128]{2,1,0:T(8,128)} custom-call(f32[64,128]{1,0:T(8,128)} %init_hbm.1, f32[4,64,128]{2,1,0:T(8,128)} %forcing_hbm.1, f32[1,64,128]{2,1,0:T(8,128)} %gain_hbm.1, f32[4096,128]{1,0:T(8,128)} %bitcast.1, f32[6,64,64]{2,1,0:T(8,128)} %faces_hbm.1, s32[6,128]{1,0:T(8,128)} %neighbor_hbm.1, s32[2,64]{1,0:T(2,128)} %send_rows_hbm.1), custom_call_target="tpu_custom_call" | custom-call | tf_op jit(solution)/shard_map/pallas_call | solution.py:321
  73.5 1.4 %fusion = (f32[1,64,128]{2,1,0:T(8,128)}, f32[1,64,128]{2,1,0:T(8,128)}) fusion(f32[2,64,128]{2,1,0:T(8,128)} %shard_map.86), kind=kLoop, calls=%fused_computation | loop fusion | bytes 131072 | tf_op jit(solution)/shard_map/slice | solution.py:360

commit v3 on v2

--- a/solution.py
+++ b/solution.py
@@ -36,10 +36,12 @@
     out_ref,
     init_ref, forcing_ref, gain_ref, inverse_ref, faces_ref, neighbor_ref, send_rows_ref,
     load_sem, res,
-    inv_t, wide, f_ref, r_ref, idx_ref,
+    inv_t, halo_inv_t, wide, f_ref, r_ref, idx_ref,
+    up_blocks, dn_blocks, below_blocks, above_blocks,
     send_up, send_dn, below, above,
     gbuf, rbuf, cbuf, cin,
     up_send, up_recv, dn_send, dn_recv,
+    ub_send, ub_recv, db_send, db_recv,
     g_send, g_recv, a_send, a_recv, c_send, c_recv,
 ):
     values, elems = init_ref.shape
@@ -112,10 +114,12 @@
     @pl.when(p == 0)
     def _():
         below[...] = jnp.zeros_like(below)
+        below_blocks[...] = jnp.zeros_like(below_blocks)
 
     @pl.when(p == ns - 1)
     def _():
         above[...] = jnp.zeros_like(above)
+        above_blocks[...] = jnp.zeros_like(above_blocks)
 
     loads[0].wait()
 
@@ -157,11 +161,11 @@
     for d in range(1, tm):
         when_scanner(lax.rem(k + d, tm), lambda d=d: to_scanner(gains, gbuf, d, g_send, g_recv).start())
 
-    def apply_inverse(vector):
+    def apply_inverse(vector, table=inv_t):
         r_ref[...] = vector
         sums = [None, None]
         for j in range(values):
-            term = inv_t[j] * r_ref[j : j + 1, :]
+            term = table[j] * r_ref[j : j + 1, :]
             sums[j % 2] = term if sums[j % 2] is None else sums[j % 2] + term
         return sums[0] + sums[1]
 
@@ -175,6 +179,23 @@
         return pltpu.make_async_remote_copy(
             src_ref=send_dn.at[s], dst_ref=above.at[s], send_sem=dn_send.at[s],
             recv_sem=dn_recv.at[s], device_id=(k, p - 1), device_id_type=MESH,
+        )
+
+    chunks = SWEEPS * steps
+    chunk = half // chunks
+
+    def up_blocks_copy(c):
+        part = pl.ds(c * chunk, chunk)
+        return pltpu.make_async_remote_copy(
+            src_ref=up_blocks.at[part], dst_ref=below_blocks.at[part], send_sem=ub_send.at[c],
+            recv_sem=ub_recv.at[c], device_id=(k, p + 1), device_id_type=MESH,
+        )
+
+    def dn_blocks_copy(c):
+        part = pl.ds(c * chunk, chunk)
+        return pltpu.make_async_remote_copy(
+            src_ref=dn_blocks.at[part], dst_ref=above_blocks.at[part], send_sem=db_send.at[c],
+            recv_sem=db_recv.at[c], device_id=(k, p - 1), device_id_type=MESH,
         )
 
     def packed(block, index):
@@ -201,14 +222,16 @@
         def _():
             dn_copy(s).wait_send()
 
-    def remainder(x, b, s):
+    def split(x):
         high = x.astype(jnp.bfloat16)
         low = (x - high.astype(jnp.float32)).astype(jnp.bfloat16)
-        stack = jnp.concatenate([high, high, low, low], axis=0)
-        along_z = jnp.dot(
-            f_ref[: 2 * values, :], stack, preferred_element_type=jnp.float32
-        )
-        minus_z, plus_z = along_z[:values], along_z[values:]
+        return jnp.concatenate([high, high, low, low], axis=0)
+
+    def z_faces(stack):
+        product = jnp.dot(f_ref[: 2 * values, :], stack, preferred_element_type=jnp.float32)
+        return product[:values], product[values:]
+
+    def send_halo(minus_z, plus_z, s):
         send_up[s] = packed(minus_z, high_index)
         send_dn[s] = packed(plus_z, low_index)
 
@@ -220,15 +243,16 @@
         def _():
             dn_copy(s).start()
 
-        along_xy = jnp.dot(
-            f_ref[2 * values :, :], stack, preferred_element_type=jnp.float32
-        )
+    def own_part(b, stack, minus_z, plus_z):
+        along_xy = jnp.dot(f_ref[2 * values :, :], stack, preferred_element_type=jnp.float32)
         rest = b - masked(pick(minus_z, own_index[4]), own_mask[4])
         rest = rest - masked(pick(plus_z, own_index[5]), own_mask[5])
         for f in range(4):
             product = along_xy[f * values : (f + 1) * values]
             rest = rest - masked(pick(product, own_index[f]), own_mask[f])
-
+        return rest
+
+    def halo(s):
         @pl.when(p < ns - 1)
         def _():
             dn_copy(s).wait_recv()
@@ -237,14 +261,68 @@
         def _():
             up_copy(s).wait_recv()
 
-        rest = rest - unpacked(below[s], halo_index[0], halo_mask[0])
-        return rest - unpacked(above[s], halo_index[1], halo_mask[1])
+        return unpacked(below[s], halo_index[0], halo_mask[0]) + unpacked(
+            above[s], halo_index[1], halo_mask[1]
+        )
+
+    def send_blocks(c):
+        def one(n, carry):
+            j = c * chunk + n
+            first, second = inv_t[j], inv_t[j + half]
+            for dst, index in ((up_blocks, high_index), (dn_blocks, low_index)):
+                for r in range(0, values, SUB):
+                    dst[j, r : r + SUB, :] = jnp.where(
+                        first_half, pick(first[r : r + SUB], index), pick(second[r : r + SUB], index)
+                    )
+            return carry
+
+        lax.fori_loop(0, chunk, one, 0, unroll=True)
+
+        @pl.when(p < ns - 1)
+        def _():
+            up_blocks_copy(c).start()
+
+        @pl.when(p > 0)
+        def _():
+            dn_blocks_copy(c).start()
+
+    def take_blocks():
+        for c in range(chunks):
+
+            @pl.when(p < ns - 1)
+            def _(c=c):
+                up_blocks_copy(c).wait_send()
+                dn_blocks_copy(c).wait_recv()
+
+            @pl.when(p > 0)
+            def _(c=c):
+                dn_blocks_copy(c).wait_send()
+                up_blocks_copy(c).wait_recv()
+
+        def one(j, carry):
+            under, over = below_blocks[j], above_blocks[j]
+            for at in (0, 1):
+                for r in range(0, values, SUB):
+                    rows_of = slice(r, r + SUB)
+                    over_part = jnp.where(
+                        halo_mask[1], pick(over[rows_of], halo_index[1] + at * layer), 0.0
+                    )
+                    halo_inv_t[j + at * half, rows_of, :] = jnp.where(
+                        halo_mask[0], pick(under[rows_of], halo_index[0] + at * layer), over_part
+                    )
+            return carry
+
+        lax.fori_loop(0, half, one, 0)
 
     def fine_step(m, field):
         b = field + forcing_ref[m]
         x = apply_inverse(b)
         for sweep in range(SWEEPS):
-            rest = remainder(x, b, sweep)
+            stack = split(x)
+            minus_z, plus_z = z_faces(stack)
+            send_halo(minus_z, plus_z, sweep)
+            send_blocks(m * SWEEPS + sweep)
+            rest = own_part(b, stack, minus_z, plus_z) - halo(sweep)
             if sweep == 0:
                 sent_halo(SWEEPS - 1, m > 0)
             else:
@@ -252,11 +330,42 @@
             x = apply_inverse(rest)
         return x
 
+    def both_sweeps(m, field):
+        base = 2 * lax.rem(m + 1, 2)
+        b = field + forcing_ref[m]
+        x = apply_inverse(b)
+        stack = split(x)
+        minus_z, plus_z = z_faces(stack)
+        send_halo(minus_z, plus_z, base)
+        inner = apply_inverse(own_part(b, stack, minus_z, plus_z))
+        inner_minus, inner_plus = z_faces(split(inner))
+        send_halo(inner_minus, inner_plus, base + 1)
+        back = jnp.concatenate(
+            [
+                jnp.where(halo_mask[0], plus_z[r : r + SUB], minus_z[r : r + SUB])
+                for r in range(0, values, SUB)
+            ],
+            axis=0,
+        )
+        back_minus, back_plus = z_faces(split(apply_inverse(back, halo_inv_t)))
+        back = masked(back_minus, halo_mask[0]) + masked(back_plus, halo_mask[1])
+        x = inner - apply_inverse(halo(base))
+        stack = split(x)
+        minus_z, plus_z = z_faces(stack)
+        rest = own_part(b, stack, minus_z, plus_z) + back
+        x = apply_inverse(rest - halo(base + 1))
+        sent_halo(base, True)
+        sent_halo(base + 1, True)
+        return x
+
     def carried_in(first):
         for d in range(1, tm):
             when_scanner(
                 lax.rem(k + d, tm), lambda d=d: to_scanner(res, rbuf, d, a_send, a_recv).start()
             )
+
+        if first:
+            take_blocks()
 
         def scan():
             rbuf[k] = res[my_rows, :]
@@ -296,9 +405,10 @@
     previous = coarse
     for iteration in range(ITERS):
         field = lax.fori_loop(
-            0, steps, fine_step, jnp.where(k == 0, init_ref[...], previous)
-        )
-        sent_halo(SWEEPS - 1, True)
+            0, steps, fine_step if iteration == 0 else both_sweeps, jnp.where(k == 0, init_ref[...], previous)
+        )
+        if iteration == 0:
+            sent_halo(SWEEPS - 1, True)
         residual = field - coarse
         res[...] = residual
         carried = carried_in(iteration == 0)
@@ -313,6 +423,7 @@
     steps = forcing.shape[0]
     scanners = min(tm, values // SUB)
     rows = values // scanners
+    chunks = SWEEPS * steps
     f32 = jnp.float32
     out = jax.ShapeDtypeStruct((2, values, elems), f32)
     vmem = pl.BlockSpec(memory_space=pltpu.VMEM)
@@ -334,19 +445,25 @@
                 dma((7,)),
                 pltpu.VMEM((values, elems), f32),
                 pltpu.VMEM((values, values, elems), f32),
+                pltpu.VMEM((values, values, elems), f32),
                 pltpu.VMEM((6 * values, 4 * values), f32),
                 pltpu.VMEM((6 * values, 4 * values), jnp.bfloat16),
                 pltpu.VMEM((values, elems), f32),
                 pltpu.VMEM((SUB, elems), jnp.int32),
-                pltpu.VMEM((2, values // 2, elems), f32),
-                pltpu.VMEM((2, values // 2, elems), f32),
-                pltpu.VMEM((2, values // 2, elems), f32),
-                pltpu.VMEM((2, values // 2, elems), f32),
+                pltpu.VMEM((values // 2, values, elems), f32),
+                pltpu.VMEM((values // 2, values, elems), f32),
+                pltpu.VMEM((values // 2, values, elems), f32),
+                pltpu.VMEM((values // 2, values, elems), f32),
+                pltpu.VMEM((4, values // 2, elems), f32),
+                pltpu.VMEM((4, values // 2, elems), f32),
+                pltpu.VMEM((4, values // 2, elems), f32),
+                pltpu.VMEM((4, values // 2, elems), f32),
                 pltpu.VMEM((tm, rows, elems), f32),
                 pltpu.VMEM((tm, rows, elems), f32),
                 pltpu.VMEM((tm, rows, elems), f32),
                 pltpu.VMEM((values, elems), f32),
-                dma((2,)), dma((2,)), dma((2,)), dma((2,)),
+                dma((4,)), dma((4,)), dma((4,)), dma((4,)),
+                dma((chunks,)), dma((chunks,)), dma((chunks,)), dma((chunks,)),
                 dma((tm,)), dma((tm,)), dma((tm,)), dma((tm,)), dma((tm,)), dma((tm,)),
             ],
             compiler_params=pltpu.CompilerParams(

time: 75.2 us -> 68.9 us (0.916)
  Pallas kernels: 72.9 us -> 66.7 us
    pallas_call x1, Pallas kernels: 72.9 us -> 66.7 us  [body(): pl.pallas_call(functools.partial(kernel, tm, ns, steps), out_shape=out, i...]
where the time goes in v3:
time: 68.9 us; the launch traced here: 68.7 us
  Pallas kernels  66.7 us (97%)
  local copies, waits for them, and re-layouts  1.4 us (2%)
    pallas_call x1, Pallas kernels, body(): pl.pallas_call(functools.partial(kernel, tm, ns, steps), out_shape=out, i...  66.7 us
    slice x1, local copies, waits for them, and re-layouts, body(): return (both[:1], both[1:])  1.4 us

profile of v3, /device:TPU:0, one launch (start us, length us, event | category | flops | bytes accessed | tf_op | source)
XLA Modules:
  0.0 68.7 jit_solution(12124406764787850633)
XLA Ops:
  0.6 66.7 %shard_map.86 = f32[2,64,128]{2,1,0:T(8,128)} custom-call(f32[64,128]{1,0:T(8,128)} %init_hbm.1, f32[4,64,128]{2,1,0:T(8,128)} %forcing_hbm.1, f32[1,64,128]{2,1,0:T(8,128)} %gain_hbm.1, f32[4096,128]{1,0:T(8,128)} %bitcast.1, f32[6,64,64]{2,1,0:T(8,128)} %faces_hbm.1, s32[6,128]{1,0:T(8,128)} %neighbor_hbm.1, s32[2,64]{1,0:T(2,128)} %send_rows_hbm.1), custom_call_target="tpu_custom_call" | custom-call | tf_op jit(solution)/shard_map/pallas_call | solution.py:432
  67.3 1.4 %fusion = (f32[1,64,128]{2,1,0:T(8,128)}, f32[1,64,128]{2,1,0:T(8,128)}) fusion(f32[2,64,128]{2,1,0:T(8,128)} %shard_map.86), kind=kLoop, calls=%fused_computation | loop fusion | bytes 131072 | tf_op jit(solution)/shard_map/slice | solution.py:477

commit v4 on v3

--- a/solution.py
+++ b/solution.py
@@ -42,6 +42,7 @@
     gbuf, rbuf, cbuf, cin,
     up_send, up_recv, dn_send, dn_recv,
     ub_send, ub_recv, db_send, db_recv,
+    fu_send, fu_recv, fd_send, fd_recv,
     g_send, g_recv, a_send, a_recv, c_send, c_recv,
 ):
     values, elems = init_ref.shape
@@ -182,17 +183,29 @@
         )
 
     chunks = SWEEPS * steps
-    chunk = half // chunks
+    chunk = half // (2 * chunks)
+    core = lax.rem(k, 2)
+    partner = k + 1 - 2 * core
+
+    def part_of(c):
+        return pl.ds(core * (half // 2) + c * chunk, chunk)
+
+    def hand_on(blocks, send, recv, c):
+        part = part_of(c)
+        return pltpu.make_async_remote_copy(
+            src_ref=blocks.at[part], dst_ref=blocks.at[part], send_sem=send.at[c],
+            recv_sem=recv.at[c], device_id=(partner, p), device_id_type=MESH,
+        )
 
     def up_blocks_copy(c):
-        part = pl.ds(c * chunk, chunk)
+        part = part_of(c)
         return pltpu.make_async_remote_copy(
             src_ref=up_blocks.at[part], dst_ref=below_blocks.at[part], send_sem=ub_send.at[c],
             recv_sem=ub_recv.at[c], device_id=(k, p + 1), device_id_type=MESH,
         )
 
     def dn_blocks_copy(c):
-        part = pl.ds(c * chunk, chunk)
+        part = part_of(c)
         return pltpu.make_async_remote_copy(
             src_ref=dn_blocks.at[part], dst_ref=above_blocks.at[part], send_sem=db_send.at[c],
             recv_sem=db_recv.at[c], device_id=(k, p - 1), device_id_type=MESH,
@@ -267,7 +280,7 @@
 
     def send_blocks(c):
         def one(n, carry):
-            j = c * chunk + n
+            j = core * (half // 2) + c * chunk + n
             first, second = inv_t[j], inv_t[j + half]
             for dst, index in ((up_blocks, high_index), (dn_blocks, low_index)):
                 for r in range(0, values, SUB):
@@ -286,18 +299,29 @@
         def _():
             dn_blocks_copy(c).start()
 
+    def share_blocks(c, also):
+        @pl.when((p < ns - 1) & also)
+        def _():
+            dn_blocks_copy(c).wait_recv()
+            hand_on(above_blocks, fd_send, fd_recv, c).start()
+
+        @pl.when((p > 0) & also)
+        def _():
+            up_blocks_copy(c).wait_recv()
+            hand_on(below_blocks, fu_send, fu_recv, c).start()
+
     def take_blocks():
         for c in range(chunks):
 
             @pl.when(p < ns - 1)
             def _(c=c):
                 up_blocks_copy(c).wait_send()
-                dn_blocks_copy(c).wait_recv()
+                hand_on(above_blocks, fd_send, fd_recv, c).wait()
 
             @pl.when(p > 0)
             def _(c=c):
                 dn_blocks_copy(c).wait_send()
-                up_blocks_copy(c).wait_recv()
+                hand_on(below_blocks, fu_send, fu_recv, c).wait()
 
         def one(j, carry):
             under, over = below_blocks[j], above_blocks[j]
@@ -322,7 +346,10 @@
             minus_z, plus_z = z_faces(stack)
             send_halo(minus_z, plus_z, sweep)
             send_blocks(m * SWEEPS + sweep)
-            rest = own_part(b, stack, minus_z, plus_z) - halo(sweep)
+            rest = own_part(b, stack, minus_z, plus_z)
+            before = m * SWEEPS + sweep - 1
+            share_blocks(jnp.maximum(before, 0), before >= 0)
+            rest = rest - halo(sweep)
             if sweep == 0:
                 sent_halo(SWEEPS - 1, m > 0)
             else:
@@ -365,7 +392,7 @@
             )
 
         if first:
-            take_blocks()
+            share_blocks(chunks - 1, True)
 
         def scan():
             rbuf[k] = res[my_rows, :]
@@ -384,6 +411,8 @@
             cin[my_rows, :] = cbuf[k]
 
         when_scanner(k, scan)
+        if first:
+            take_blocks()
         for d in range(1, tm):
 
             def sent(d=d):
@@ -464,6 +493,7 @@
                 pltpu.VMEM((values, elems), f32),
                 dma((4,)), dma((4,)), dma((4,)), dma((4,)),
                 dma((chunks,)), dma((chunks,)), dma((chunks,)), dma((chunks,)),
+                dma((chunks,)), dma((chunks,)), dma((chunks,)), dma((chunks,)),
                 dma((tm,)), dma((tm,)), dma((tm,)), dma((tm,)), dma((tm,)), dma((tm,)),
             ],
             compiler_params=pltpu.CompilerParams(

time: 68.9 us -> 66.8 us (0.970)
  Pallas kernels: 66.7 us -> 64.6 us
    pallas_call x1, Pallas kernels: 66.7 us -> 64.6 us  [body(): pl.pallas_call(functools.partial(kernel, tm, ns, steps), out_shape=out, i...]
where the time goes in v4:
time: 66.8 us; the launch traced here: 66.6 us
  Pallas kernels  64.6 us (97%)
  local copies, waits for them, and re-layouts  1.4 us (2%)
    pallas_call x1, Pallas kernels, body(): pl.pallas_call(functools.partial(kernel, tm, ns, steps), out_shape=out, i...  64.6 us
    slice x1, local copies, waits for them, and re-layouts, body(): return (both[:1], both[1:])  1.4 us

profile of v4, /device:TPU:0, one launch (start us, length us, event | category | flops | bytes accessed | tf_op | source)
XLA Modules:
  0.0 66.6 jit_solution(5043174394918500925)
XLA Ops:
  0.6 64.6 %shard_map.86 = f32[2,64,128]{2,1,0:T(8,128)} custom-call(f32[64,128]{1,0:T(8,128)} %init_hbm.1, f32[4,64,128]{2,1,0:T(8,128)} %forcing_hbm.1, f32[1,64,128]{2,1,0:T(8,128)} %gain_hbm.1, f32[4096,128]{1,0:T(8,128)} %bitcast.1, f32[6,64,64]{2,1,0:T(8,128)} %faces_hbm.1, s32[6,128]{1,0:T(8,128)} %neighbor_hbm.1, s32[2,64]{1,0:T(2,128)} %send_rows_hbm.1), custom_call_target="tpu_custom_call" | custom-call | tf_op jit(solution)/shard_map/pallas_call | solution.py:461
  65.2 1.4 %fusion = (f32[1,64,128]{2,1,0:T(8,128)}, f32[1,64,128]{2,1,0:T(8,128)}) fusion(f32[2,64,128]{2,1,0:T(8,128)} %shard_map.86), kind=kLoop, calls=%fused_computation | loop fusion | bytes 131072 | tf_op jit(solution)/shard_map/slice | solution.py:507

commit v5 on v4

--- a/solution.py
+++ b/solution.py
@@ -33,7 +33,7 @@
 def kernel(
     tm, ns, steps,
     init_hbm, forcing_hbm, gain_hbm, inverse_hbm, faces_hbm, neighbor_hbm, send_rows_hbm,
-    out_ref,
+    coarse_ref, residual_ref,
     init_ref, forcing_ref, gain_ref, inverse_ref, faces_ref, neighbor_ref, send_rows_ref,
     load_sem, res,
     inv_t, halo_inv_t, wide, f_ref, r_ref, idx_ref,
@@ -89,7 +89,7 @@
         part = faces_ref[(4, 5, 0, 1, 2, 3)[f]]
         high = part.astype(jnp.bfloat16).astype(jnp.float32)
         low = part - high
-        for c, piece in enumerate((high, low, high, low)):
+        for c, piece in enumerate((high, low, high)):
             wide[f * values : (f + 1) * values, c * values : (c + 1) * values] = piece
     f_ref[...] = wide[...].astype(jnp.bfloat16)
 
@@ -238,7 +238,7 @@
     def split(x):
         high = x.astype(jnp.bfloat16)
         low = (x - high.astype(jnp.float32)).astype(jnp.bfloat16)
-        return jnp.concatenate([high, high, low, low], axis=0)
+        return jnp.concatenate([high, high, low], axis=0)
 
     def z_faces(stack):
         product = jnp.dot(f_ref[: 2 * values, :], stack, preferred_element_type=jnp.float32)
@@ -336,7 +336,7 @@
                     )
             return carry
 
-        lax.fori_loop(0, half, one, 0)
+        lax.fori_loop(0, half, one, 0, unroll=8)
 
     def fine_step(m, field):
         b = field + forcing_ref[m]
@@ -443,8 +443,8 @@
         carried = carried_in(iteration == 0)
         previous = previous + carried
         coarse = coarse + (gain_ref[0] * carried + residual)
-    out_ref[0] = coarse
-    out_ref[1] = residual
+    coarse_ref[0] = coarse
+    residual_ref[0] = residual
 
 
 def body(tm, ns, initial_state, forcing, coarse_gain, block_inverse, face_blocks, neighbor, send_rows):
@@ -454,15 +454,15 @@
     rows = values // scanners
     chunks = SWEEPS * steps
     f32 = jnp.float32
-    out = jax.ShapeDtypeStruct((2, values, elems), f32)
+    out = jax.ShapeDtypeStruct((1, values, elems), f32)
     vmem = pl.BlockSpec(memory_space=pltpu.VMEM)
     dma = pltpu.SemaphoreType.DMA
-    both = (
+    return tuple(
         pl.pallas_call(
             functools.partial(kernel, tm, ns, steps),
-            out_shape=out,
+            out_shape=(out, out),
             in_specs=[pl.BlockSpec(memory_space=pl.ANY)] * 7,
-            out_specs=vmem,
+            out_specs=(vmem, vmem),
             scratch_shapes=[
                 pltpu.VMEM((values, elems), f32),
                 pltpu.VMEM(forcing.shape, f32),
@@ -475,8 +475,8 @@
                 pltpu.VMEM((values, elems), f32),
                 pltpu.VMEM((values, values, elems), f32),
                 pltpu.VMEM((values, values, elems), f32),
-                pltpu.VMEM((6 * values, 4 * values), f32),
-                pltpu.VMEM((6 * values, 4 * values), jnp.bfloat16),
+                pltpu.VMEM((6 * values, 3 * values), f32),
+                pltpu.VMEM((6 * values, 3 * values), jnp.bfloat16),
                 pltpu.VMEM((values, elems), f32),
                 pltpu.VMEM((SUB, elems), jnp.int32),
                 pltpu.VMEM((values // 2, values, elems), f32),
@@ -504,7 +504,6 @@
             block_inverse.reshape(values * values, elems), face_blocks, neighbor, send_rows,
         )
     )
-    return both[:1], both[1:]
 
 
 def solution(mesh):

time: 66.8 us -> 67.1 us (level)
  local copies, waits for them, and re-layouts: 1.4 us -> 2.75 us
  Pallas kernels: 64.6 us -> 63.4 us
    unnamed x0 -> x2, local copies, waits for them, and re-layouts: none -> 2.75 us
    slice x1 -> x0, local copies, waits for them, and re-layouts: 1.4 us -> none  [body(): return (both[:1], both[1:])]
    pallas_call x1, Pallas kernels: 64.6 us -> 63.4 us  [body(): pl.pallas_call(functools.partial(kernel, tm, ns, steps), out_shape=(out,...]
where the time goes in v5:
time: 67.1 us; the launch traced here: 66.8 us
  Pallas kernels  63.4 us (94%)
  local copies, waits for them, and re-layouts  2.75 us (4%)
    pallas_call x1, Pallas kernels, body(): pl.pallas_call(functools.partial(kernel, tm, ns, steps), out_shape=(out,...  63.4 us
    unnamed x2, local copies, waits for them, and re-layouts  2.75 us

profile of v5, /device:TPU:0, one launch (start us, length us, event | category | flops | bytes accessed | tf_op | source)
XLA Modules:
  0.0 66.8 jit_solution(11333605304297085825)
XLA Ops:
  0.6 63.4 %shard_map.86 = (f32[1,64,128]{2,1,0:T(8,128)}, f32[1,64,128]{2,1,0:T(8,128)}) custom-call(f32[64,128]{1,0:T(8,128)} %init_hbm.1, f32[4,64,128]{2,1,0:T(8,128)} %forcing_hbm.1, f32[1,64,128]{2,1,0:T(8,128)} %gain_hbm.1, f32[4096,128]{1,0:T(8,128)} %bitcast.1, f32[6,64,64]{2,1,0:T(8,128)} %faces_hbm.1, s32[6,128]{1,0:T(8,128)} %neighbor_hbm.1, ...), custom_call_target="tpu_custom_call" | custom-call | tf_op jit(solution)/shard_map/pallas_call | solution.py:461
  64.1 1.4 %copy.11 = f32[1,64,128]{2,1,0:T(8,128)} copy(f32[1,64,128]{2,1,0:T(8,128)} %get-tuple-element.4) | data formatting | bytes 65536
  65.4 1.4 %copy.12 = f32[1,64,128]{2,1,0:T(8,128)} copy(f32[1,64,128]{2,1,0:T(8,128)} %get-tuple-element.5) | data formatting | bytes 65536

commit v6 on v4

--- a/solution.py
+++ b/solution.py
@@ -89,7 +89,7 @@
         part = faces_ref[(4, 5, 0, 1, 2, 3)[f]]
         high = part.astype(jnp.bfloat16).astype(jnp.float32)
         low = part - high
-        for c, piece in enumerate((high, low, high, low)):
+        for c, piece in enumerate((high, low, high)):
             wide[f * values : (f + 1) * values, c * values : (c + 1) * values] = piece
     f_ref[...] = wide[...].astype(jnp.bfloat16)
 
@@ -129,7 +129,7 @@
             inv_t[j, pl.ds(i, SUB), :] = inverse_ref[pl.ds(i * values + j, SUB, stride=values), :]
         return carry
 
-    lax.fori_loop(0, values, turn, 0, unroll=4)
+    lax.fori_loop(0, values, turn, 0, unroll=8)
 
     expected = tm - 1 + (p > 0).astype(jnp.int32) + (p < ns - 1).astype(jnp.int32)
     pl.semaphore_wait(barrier, expected)
@@ -238,7 +238,7 @@
     def split(x):
         high = x.astype(jnp.bfloat16)
         low = (x - high.astype(jnp.float32)).astype(jnp.bfloat16)
-        return jnp.concatenate([high, high, low, low], axis=0)
+        return jnp.concatenate([high, high, low], axis=0)
 
     def z_faces(stack):
         product = jnp.dot(f_ref[: 2 * values, :], stack, preferred_element_type=jnp.float32)
@@ -336,7 +336,7 @@
                     )
             return carry
 
-        lax.fori_loop(0, half, one, 0)
+        lax.fori_loop(0, half, one, 0, unroll=8)
 
     def fine_step(m, field):
         b = field + forcing_ref[m]
@@ -475,8 +475,8 @@
                 pltpu.VMEM((values, elems), f32),
                 pltpu.VMEM((values, values, elems), f32),
                 pltpu.VMEM((values, values, elems), f32),
-                pltpu.VMEM((6 * values, 4 * values), f32),
-                pltpu.VMEM((6 * values, 4 * values), jnp.bfloat16),
+                pltpu.VMEM((6 * values, 3 * values), f32),
+                pltpu.VMEM((6 * values, 3 * values), jnp.bfloat16),
                 pltpu.VMEM((values, elems), f32),
                 pltpu.VMEM((SUB, elems), jnp.int32),
                 pltpu.VMEM((values // 2, values, elems), f32),

time: 66.8 us -> 65.6 us (0.982)
  Pallas kernels: 64.6 us -> 63.3 us
    pallas_call x1, Pallas kernels: 64.6 us -> 63.3 us  [body(): pl.pallas_call(functools.partial(kernel, tm, ns, steps), out_shape=out, i...]
where the time goes in v6:
time: 65.6 us; the launch traced here: 65.3 us
  Pallas kernels  63.3 us (96%)
  local copies, waits for them, and re-layouts  1.4 us (2%)
    pallas_call x1, Pallas kernels, body(): pl.pallas_call(functools.partial(kernel, tm, ns, steps), out_shape=out, i...  63.3 us
    slice x1, local copies, waits for them, and re-layouts, body(): return (both[:1], both[1:])  1.4 us

profile of v6, /device:TPU:0, one launch (start us, length us, event | category | flops | bytes accessed | tf_op | source)
XLA Modules:
  0.0 65.3 jit_solution(12027984005408702851)
XLA Ops:
  0.6 63.3 %shard_map.86 = f32[2,64,128]{2,1,0:T(8,128)} custom-call(f32[64,128]{1,0:T(8,128)} %init_hbm.1, f32[4,64,128]{2,1,0:T(8,128)} %forcing_hbm.1, f32[1,64,128]{2,1,0:T(8,128)} %gain_hbm.1, f32[4096,128]{1,0:T(8,128)} %bitcast.1, f32[6,64,64]{2,1,0:T(8,128)} %faces_hbm.1, s32[6,128]{1,0:T(8,128)} %neighbor_hbm.1, s32[2,64]{1,0:T(2,128)} %send_rows_hbm.1), custom_call_target="tpu_custom_call" | custom-call | tf_op jit(solution)/shard_map/pallas_call | solution.py:461
  63.9 1.4 %fusion = (f32[1,64,128]{2,1,0:T(8,128)}, f32[1,64,128]{2,1,0:T(8,128)}) fusion(f32[2,64,128]{2,1,0:T(8,128)} %shard_map.86), kind=kLoop, calls=%fused_computation | loop fusion | bytes 131072 | tf_op jit(solution)/shard_map/slice | solution.py:507

commit v7 on v6

--- a/solution.py
+++ b/solution.py
@@ -157,6 +157,7 @@
             device_id=(place, p), device_id_type=MESH,
         )
 
+    far_first = sorted(range(1, tm), key=lambda d: -min(d, tm - d))
     my_rows = pl.ds(pl.multiple_of(lax.rem(k, scanners) * rows, SUB), rows)
     gains = gain_ref.at[0]
     for d in range(1, tm):
@@ -386,7 +387,7 @@
         return x
 
     def carried_in(first):
-        for d in range(1, tm):
+        for d in far_first:
             when_scanner(
                 lax.rem(k + d, tm), lambda d=d: to_scanner(res, rbuf, d, a_send, a_recv).start()
             )
@@ -406,7 +407,7 @@
             for lap in range(tm):
                 cbuf[lap] = running
                 running = gbuf[lap] * running + rbuf[lap]
-            for d in range(1, tm):
+            for d in far_first:
                 from_scanner(d).start()
             cin[my_rows, :] = cbuf[k]
 

time: 65.6 us -> 65.6 us (level)
  no operation moved by 1% of the time
where the time goes in v7:
time: 65.6 us; the launch traced here: 65.4 us
  Pallas kernels  63.3 us (96%)
  local copies, waits for them, and re-layouts  1.4 us (2%)
    pallas_call x1, Pallas kernels, body(): pl.pallas_call(functools.partial(kernel, tm, ns, steps), out_shape=out, i...  63.3 us
    slice x1, local copies, waits for them, and re-layouts, body(): return (both[:1], both[1:])  1.4 us

profile of v7, /device:TPU:0, one launch (start us, length us, event | category | flops | bytes accessed | tf_op | source)
XLA Modules:
  0.0 65.4 jit_solution(10623429556528917636)
XLA Ops:
  0.6 63.3 %shard_map.86 = f32[2,64,128]{2,1,0:T(8,128)} custom-call(f32[64,128]{1,0:T(8,128)} %init_hbm.1, f32[4,64,128]{2,1,0:T(8,128)} %forcing_hbm.1, f32[1,64,128]{2,1,0:T(8,128)} %gain_hbm.1, f32[4096,128]{1,0:T(8,128)} %bitcast.1, f32[6,64,64]{2,1,0:T(8,128)} %faces_hbm.1, s32[6,128]{1,0:T(8,128)} %neighbor_hbm.1, s32[2,64]{1,0:T(2,128)} %send_rows_hbm.1), custom_call_target="tpu_custom_call" | custom-call | tf_op jit(solution)/shard_map/pallas_call | solution.py:462
  64.0 1.4 %fusion = (f32[1,64,128]{2,1,0:T(8,128)}, f32[1,64,128]{2,1,0:T(8,128)}) fusion(f32[2,64,128]{2,1,0:T(8,128)} %shard_map.86), kind=kLoop, calls=%fused_computation | loop fusion | bytes 131072 | tf_op jit(solution)/shard_map/slice | solution.py:508
